TPU v7x, 32 devices: a whole 2x2x4 slice. The times are simulated.
32 devices in a mesh: grp: 4 (over x, core), shard: 8 (over z, y).
Axes of the slice: x: 2, y: 2, z: 4, core: 2. Of those that a mesh axis runs over, the one named last changes fastest.
Arguments:
- inputs: bfloat16 [2, 1024, 4096], P(None, None, 'grp'), may hold values from -6 to 6
- up_cotangent: bfloat16 [2, 1024, 14336], P(None, None, 'shard'), may hold values from -0.1875 to 0.1875
- signs: int32 [4096, 16384], P('grp', 'shard'), may hold values from -1 to 1, as said below
- kept_row: int32 [8192], replicated, may hold values from 0 to 4095
- kept_col: int32 [8192], replicated, may hold values from 0 to 16383
Outputs:
- features: float32 [2, 8192], P(None, ('grp', 'shard'))
Inputs may be any that keep to these rules, and one draw needn't show every extreme that they name: `signs`: every entry is -1 or +1.
All inputs are finite; a program needn't handle non-finite values.
Results may differ from a plain program's by a relative error of at most 0.0003.
Values sent between devices are 32-bit elements; how exact they have to be, the bound alone decides.
No kernel may reach another device: no remote copies, remote signals or barrier semaphores. Data moves between devices by JAX's collectives and lax.ppermute only.
A program may use at most 320 MiB of HBM per device.

v0:
```python
import math

import jax
import jax.numpy as jnp
from jax import lax
from jax.sharding import PartitionSpec as P

D = 4096
FPAD = 16384


def partner_2(block, axis, apart):
    count = lax.axis_size(axis)
    route = []
    for low in range(count):
        high = low | 1 << apart
        if high != low and high < count:
            route += [(low, high), (high, low)]
    return lax.ppermute(block, axis, route)


def hadamard_table(length):
    indices = jnp.arange(length, dtype=jnp.int32)
    parity = jnp.zeros((length, length), jnp.int32)
    for bit_number in range(length.bit_length() - 1):
        left_bits = jnp.bitwise_and(jnp.right_shift(indices, bit_number), 1)
        parity = parity + left_bits[:, None] * left_bits[None, :]
    return (1 - 2 * (parity % 2)).astype(jnp.float32)


def local(inputs, up_cotangent, signs, kept_row, kept_col):
    examples = inputs.shape[0]
    row_count = inputs.shape[2]
    unit_count = up_cotangent.shape[2]
    column_count = signs.shape[1]
    scale = 1.0 / math.sqrt(D * FPAD)
    gradient = jnp.einsum("etd,etf->edf", inputs, up_cotangent, preferred_element_type=jnp.float32)
    placed = jnp.pad(gradient, ((0, 0), (0, 0), (0, column_count - unit_count)))
    values = placed * signs.astype(jnp.float32)[None]
    row_table = hadamard_table(row_count)
    column_table = hadamard_table(column_count)
    values = jnp.einsum("ir,erc->eic", row_table, values, precision=lax.Precision.HIGHEST)
    values = jnp.einsum("erc,cj->erj", values, column_table, precision=lax.Precision.HIGHEST)
    position = lax.axis_index("shard")
    for bit_number in range(lax.axis_size("shard").bit_length() - 1):
        partner = partner_2(values, "shard", bit_number)
        upper_half = jnp.bitwise_and(jnp.right_shift(position, bit_number), 1) == 1
        values = jnp.where(upper_half, partner - values, values + partner)
    position = lax.axis_index("grp")
    for bit_number in range(lax.axis_size("grp").bit_length() - 1):
        partner = partner_2(values, "grp", bit_number)
        upper_half = jnp.bitwise_and(jnp.right_shift(position, bit_number), 1) == 1
        values = jnp.where(upper_half, partner - values, values + partner)
    local_row = kept_row - lax.axis_index("grp") * row_count
    local_col = kept_col - lax.axis_index("shard") * column_count
    inside = (
        (local_row >= 0) & (local_row < row_count) & (local_col >= 0) & (local_col < column_count)
    )
    flat_index = jnp.clip(local_row, 0, row_count - 1) * column_count + jnp.clip(
        local_col, 0, column_count - 1
    )
    picked = jnp.take(values.reshape(examples, row_count * column_count), flat_index, axis=1)
    share_term = jnp.where(inside[None, :], picked, 0.0) * scale
    return lax.psum_scatter(share_term, ("grp", "shard"), scatter_dimension=1, tiled=True)


def solution(mesh):
    placed = (P(None, None, "grp"), P(None, None, "shard"), P("grp", "shard"), P(), P())
    return jax.shard_map(
        local, mesh=mesh, in_specs=placed, out_specs=P(None, ("grp", "shard")), check_vma=False
    )
```

profile of v0, /device:TPU:0, one launch (start us, length us, event | category | flops | bytes accessed | tf_op | source)
XLA Modules:
  0.0 2593.2 jit_solution(11000233172414715135)
XLA Ops:
  6.7 0.0 slice-start.1
  6.7 4.4 convert_element_type.11
  11.1 0.0 slice-done
  11.1 1.0 copy-done.2
  12.1 1.2 slice-done.1
  13.3 11.2 fusion.79
  24.5 11.0 fusion.93
  35.5 72.3 %fusion.8 = f32[2,2048,1024]{1,2,0:T(8,128)} fusion(s32[1024]{0:T(1024)S(1)} %get-tuple-element.7, s32[1024]{0:T(1024)S(1)} %get-tuple-element.8, s32[1024]{0:T(1024)S(1)} %get-tuple-element.9, s32[1024]{0:T(1024)S(1)} %get-tuple-element.10, s32[1024]{0:T(1024)S(1)} %get-tuple-element.11, s32[1024]{0:T(1024)S(1)} %get-tuple-element.12, ...), kind=kOutput, calls=%fused_computation.16 | convolution fusion | flops 51574210560 | bytes 33595392 | tf_op jit(solution)/shard_map/ir,erc->eic/dot_general | solution.py:42
  107.8 23.5 fusion.91
  131.3 114.9 %fusion.5 = f32[2,1024,2048]{2,1,0:T(8,128)} fusion(f32[2,2048,1024]{1,2,0:T(8,128)} %fusion.8, f32[2048,2048,1]{1,0,2:T(8,128)} %fusion.91), kind=kOutput, calls=%fused_computation.9 | convolution fusion | flops 103079215104 | bytes 50331648 | tf_op jit(solution)/shard_map/erc,cj->erj/dot_general | solution.py:43
  246.3 3.0 collective-permute-start
  249.2 360.5 %collective-permute-done = f32[2,1024,2048]{2,1,0:T(8,128)} collective-permute-done((f32[2,1024,2048]{2,1,0:T(8,128)}, f32[2,1024,2048]{2,1,0:T(8,128)}, u32[]{:S(2)}, u32[]{:S(2)}) %collective-permute-start) | collective-permute-done | bytes 16777248 | tf_op jit(solution)/shard_map/ppermute | solution.py:19
  609.8 16.9 add_select_fusion.4
  626.7 1.8 collective-permute-start.1
  628.5 359.9 %collective-permute-done.1 = f32[2,1024,2048]{2,1,0:T(8,128)} collective-permute-done((f32[2,1024,2048]{2,1,0:T(8,128)}, f32[2,1024,2048]{2,1,0:T(8,128)}, u32[]{:S(2)}, u32[]{:S(2)}) %collective-permute-start.1) | collective-permute-done | bytes 16777248 | tf_op jit(solution)/shard_map/ppermute | solution.py:19
  988.4 16.9 add_select_fusion.3
  1005.4 2.5 collective-permute-start.2
  1007.9 718.7 %collective-permute-done.2 = f32[2,1024,2048]{2,1,0:T(8,128)} collective-permute-done((f32[2,1024,2048]{2,1,0:T(8,128)}, f32[2,1024,2048]{2,1,0:T(8,128)}, u32[]{:S(2)}, u32[]{:S(2)}) %collective-permute-start.2) | collective-permute-done | bytes 16777248 | tf_op jit(solution)/shard_map/ppermute | solution.py:19
  1726.6 17.2 add_select_fusion.2
  1743.8 0.0 collective-permute-start.3
  1743.8 25.5 collective-permute-done.3
  1769.2 16.9 add_select_fusion.1
  1786.2 1.1 collective-permute-start.4
  1787.3 361.4 %collective-permute-done.4 = f32[2,1024,2048]{2,1,0:T(8,128)} collective-permute-done((f32[2,1024,2048]{2,1,0:T(8,128)}, f32[2,1024,2048]{2,1,0:T(8,128)}, u32[]{:S(2)}, u32[]{:S(2)}) %collective-permute-start.4) | collective-permute-done | bytes 16777248 | tf_op jit(solution)/shard_map/ppermute | solution.py:19
  2148.8 11.8 select_bitcast_fusion
  2160.5 21.3 copy.8
  2181.9 252.7 %gather_fusion = f32[8192,2]{0,1:T(2,128)S(1)} fusion(f32[2,2097152]{1,0:T(2,128)} %bitcast.27, s32[8192]{0:T(1024)S(1)} %broadcast_clamp_fusion), kind=kCustom, calls=%fused_computation | custom fusion | bytes 163840 | tf_op jit(solution)/shard_map/jit(_take)/gather | solution.py:62
  2434.6 0.1 multiply_bitcast_fusion
  2434.7 2.6 copy.6
  2437.3 0.0 reduce-scatter.4.cloned.1.call-update
  2437.3 147.1 %reduce-scatter.4.cloned.1.call-done = f32[256,2]{1,0:T(8,128)} async-done(((f32[8192,2]{1,0:T(8,128)}), f32[256,2]{1,0:T(8,128)}) %reduce-scatter.4.cloned.1.call-update) | async-done | bytes 2064
  2584.4 1.6 copy.7
  (21 shorter events, 0.1 us)
Async XLA Ops:
  6.5 4.5 slice-start
  6.5 2577.9 %reduce-scatter.4.cloned.1.call-start = ((), (), s32[]{:S(2)}) async-start(), calls=%async_computation.1 | async-start | bytes 4325376
  6.5 5.5 copy-start.2
  6.7 6.6 slice-start.1
  246.3 363.5 %collective-permute-start = (f32[2,1024,2048]{2,1,0:T(8,128)}, f32[2,1024,2048]{2,1,0:T(8,128)}, u32[]{:S(2)}, u32[]{:S(2)}) collective-permute-start(f32[2,1024,2048]{2,1,0:T(8,128)} %fusion.5), channel_id=1, source_target_pairs={{0,1},{1,0},{2,3},{3,2},{4,5},{5,4},{6,7},{7,6},{8,9},{9,8},{10,11... | collective-permute-start | bytes 50331656 | tf_op jit(solution)/shard_map/ppermute | solution.py:19
  626.7 361.7 %collective-permute-start.1 = (f32[2,1024,2048]{2,1,0:T(8,128)}, f32[2,1024,2048]{2,1,0:T(8,128)}, u32[]{:S(2)}, u32[]{:S(2)}) collective-permute-start(f32[2,1024,2048]{2,1,0:T(8,128)} %add_select_fusion.4), channel_id=1, source_target_pairs={{0,2},{2,0},{1,3},{3,1},{4,6},{6,4},{5,7},{7,5},{8,10},{10,8},{9,1... | collective-permute-start | bytes 50331656 | tf_op jit(solution)/shard_map/ppermute | solution.py:19
  1005.4 721.2 %collective-permute-start.2 = (f32[2,1024,2048]{2,1,0:T(8,128)}, f32[2,1024,2048]{2,1,0:T(8,128)}, u32[]{:S(2)}, u32[]{:S(2)}) collective-permute-start(f32[2,1024,2048]{2,1,0:T(8,128)} %add_select_fusion.3), channel_id=1, source_target_pairs={{0,4},{4,0},{1,5},{5,1},{2,6},{6,2},{3,7},{7,3},{8,12},{12,8},{9,1... | collective-permute-start | bytes 50331656 | tf_op jit(solution)/shard_map/ppermute | solution.py:19
  1743.8 25.5 collective-permute-start.3
  1743.8 43.5 %copy-start = (s32[8192]{0:T(1024)S(1)}, s32[8192]{0:T(1024)}, u32[]{:S(2)}) copy-start(s32[8192]{0:T(1024)} %param.9) | copy-start | bytes 98308
  1743.8 43.5 %copy-start.1 = (s32[8192]{0:T(1024)S(1)}, s32[8192]{0:T(1024)}, u32[]{:S(2)}) copy-start(s32[8192]{0:T(1024)} %param.8) | copy-start | bytes 98308
  1786.2 362.6 %collective-permute-start.4 = (f32[2,1024,2048]{2,1,0:T(8,128)}, f32[2,1024,2048]{2,1,0:T(8,128)}, u32[]{:S(2)}, u32[]{:S(2)}) collective-permute-start(f32[2,1024,2048]{2,1,0:T(8,128)} %add_select_fusion.1), channel_id=1, source_target_pairs={{0,16},{16,0},{8,24},{24,8},{1,17},{17,1},{9,25},{25,9},{2,18},{18... | collective-permute-start | bytes 50331656 | tf_op jit(solution)/shard_map/ppermute | solution.py:19
Sparse Core Ops, SparseCore 0:
  2437.4 146.9 reduce-scatter.3
where the time goes:
time: 2600 us; the launch traced here: 2590 us
  waiting for transfers between devices  1970 us (76%)
  local copies, waits for them, and re-layouts  280 us (11%)
  matrix products  198 us (8%)
  other arithmetic  119 us (5%)
    ppermute x5, waiting for transfers between devices, partner_2(): return lax.ppermute(block, axis, route)  1830 us
    gather x1, local copies, waits for them, and re-layouts, local(): jnp.take(values.reshape(examples, row_count * column_count), flat_index,...  253 us
    unnamed x2, waiting for transfers between devices  147 us
    dot_general x1, matrix products, local(): jnp.einsum('erc,cj->erj', values, column_table, precision=lax.Precision.H...  115 us
    dot_general x1, matrix products, local(): jnp.einsum('ir,erc->eic', row_table, values, precision=lax.Precision.HIGH...  72.3 us
    select_n x4, other arithmetic, local(): values = jnp.where(upper_half, partner - values, values + partner)  67.9 us
  transfers between devices with their start and end apart: 6, of which 6 were waited for; matrix products, arithmetic and copies ran while one was open for 0% of the time, Pallas kernels for 0%

commit v1 on v0

v1 whole, which is shorter than its diff:
```python
import math

import jax
import jax.numpy as jnp
import numpy as np
from jax import lax
from jax.experimental import pallas as pl
from jax.experimental.pallas import tpu as pltpu
from jax.sharding import PartitionSpec as P

D = 4096
FPAD = 16384
LANES = 128
TILE = 256


def hadamard(length):
    table = np.ones((1, 1), np.float32)
    while table.shape[0] < length:
        table = np.block([[table, table], [table, -table]])
    return table


def interleaved_table():
    h = hadamard(LANES)
    table = np.zeros((LANES, 2, 2, LANES), np.float32)
    table[:, 0, 0, :] = h
    table[:, 1, 1, :] = h
    return table.reshape(2 * LANES, 2 * LANES)


def butterflies(blocks):
    blocks = list(blocks)
    width = 1
    while width < len(blocks):
        for low in range(len(blocks)):
            if low & width:
                continue
            a, b = blocks[low], blocks[low | width]
            if b is None:
                blocks[low | width] = a
            else:
                blocks[low], blocks[low | width] = a + b, a - b
        width *= 2
    return blocks


def split(values):
    high = values.astype(jnp.bfloat16)
    low = (values - high.astype(jnp.float32)).astype(jnp.bfloat16)
    return high, low


def parity_sign(bits):
    for shift in (16, 8, 4, 2, 1):
        bits = jnp.bitwise_xor(bits, jnp.right_shift(bits, shift))
    return (1 - 2 * jnp.bitwise_and(bits, 1)).astype(jnp.float32)


def sketch_kernel(row_count, column_count, tiles,
                  position_ref, x_ref, u_ref, signs_ref, kept_row_ref, kept_col_ref, row_table_ref, lane_table_ref,
                  out_ref,
                  xt, signed, table, spot_vmem, spot_smem, stage_a, stage_b, spot_sem):
    step = pl.program_id(0)
    row_blocks = row_count // LANES
    column_blocks = column_count // LANES
    pairs = column_blocks // 2
    chunks = kept_row_ref.shape[0]
    f32 = jnp.float32

    def spot_copy():
        return pltpu.make_async_copy(spot_vmem, spot_smem, spot_sem)

    @pl.when(step == 0)
    def _():
        row = jnp.bitwise_and(kept_row_ref[...], row_count - 1)
        col = jnp.bitwise_and(kept_col_ref[...], column_count - 1)
        block = (row // LANES) * column_blocks + col // LANES
        spot_vmem[...] = (block * LANES + jnp.bitwise_and(row, LANES - 1)) * 2
        spot_copy().start()
        for e in range(2):
            for block in range(row_blocks):
                cut = slice(block * LANES, (block + 1) * LANES)
                xt[e, cut, :] = x_ref[e, :, cut].T

    for block in range(row_blocks):
        cut = slice(block * LANES, (block + 1) * LANES)
        block_signs = signs_ref[cut, :].astype(f32)
        for e in range(2):
            product = jnp.dot(xt[e, cut, :], u_ref[e], preferred_element_type=f32)
            signed[block, e * LANES:(e + 1) * LANES, :] = product * block_signs

    group = 16
    for start in range(0, 2 * LANES, group):
        rows = slice(start, start + group)
        blocks = butterflies([signed[block, rows, :] for block in range(row_blocks)])
        for block in range(row_blocks):
            signed[block, rows, :] = blocks[block]

    for block in range(row_blocks):
        high, low = split(signed[block])
        whole = jnp.dot(row_table_ref[...], high, preferred_element_type=f32)
        whole += jnp.dot(row_table_ref[...], low, preferred_element_type=f32)
        left, right = whole[:, :LANES], whole[:, LANES:]
        base = pl.multiple_of((block * column_blocks + 2 * step) * TILE, TILE)
        table[pl.ds(base, TILE), :] = left + right
        table[pl.ds(base + TILE, TILE), :] = left - right

    @pl.when(step == tiles - 1)
    def _():
        if pairs > 1:
            part = 32

            def columns(at, carry):
                block = at // (TILE // part)
                row = (at % (TILE // part)) * part
                base = pl.multiple_of(block * (column_blocks * TILE) + row, 8)
                for half in range(2):
                    for extra in range(0, part, 8):
                        def place(pair):
                            return pl.ds(base + (2 * pair + half) * TILE + extra, 8)

                        blocks = butterflies(
                            [table[place(pair), :] if pair < tiles else None for pair in range(pairs)])
                        for pair in range(pairs):
                            table[place(pair), :] = blocks[pair]
                return carry

            lax.fori_loop(0, row_blocks * (TILE // part), columns, 0)
        spot_copy().wait()

        def gather(chunk, stage):
            for u in range(LANES):
                at = pl.multiple_of(spot_smem[chunk, u], 2)
                stage[2 * u:2 * u + 2, :] = table[pl.ds(at, 2), :]

        lane_table = lane_table_ref[...]
        scale = 1.0 / math.sqrt(D * FPAD)

        def finish(chunk, stage):
            rows = jnp.concatenate([stage[pl.ds(0, LANES, stride=2), :], stage[pl.ds(1, LANES, stride=2), :]], axis=0)
            high, low = split(rows)
            both = jnp.concatenate([high, low], axis=1)
            whole = lax.dot_general(lane_table, both, (((1,), (1,)), ((), ())), preferred_element_type=f32)
            kept_row = kept_row_ref[pl.ds(chunk, 1), :]
            kept_col = kept_col_ref[pl.ds(chunk, 1), :]
            lane = jnp.bitwise_and(kept_col, LANES - 1)
            sign = scale * parity_sign(jnp.bitwise_xor(
                jnp.bitwise_and(kept_row // row_count, position_ref[0]),
                jnp.bitwise_and(kept_col // column_count, position_ref[1])))
            mask = lax.broadcasted_iota(jnp.int32, (LANES, LANES), 0) == lane
            for e in range(2):
                picked = jnp.where(mask, whole[:, e * LANES:(e + 1) * LANES], 0.0)
                out_ref[e, pl.ds(chunk, 1), :] = jnp.sum(picked, axis=0, keepdims=True) * sign

        gather(0, stage_a)

        def two_chunks(at, carry):
            gather(2 * at + 1, stage_b)
            finish(2 * at, stage_a)
            gather(jnp.minimum(2 * at + 2, chunks - 1), stage_a)
            finish(2 * at + 1, stage_b)
            return carry

        lax.fori_loop(0, chunks // 2, two_chunks, 0)


def partial_features(position, inputs, up_cotangent, signs, kept_row, kept_col):
    examples, depth, row_count = inputs.shape
    column_count = signs.shape[1]
    if up_cotangent.shape[2] % TILE:
        extra = -up_cotangent.shape[2] % TILE
        up_cotangent = jnp.pad(up_cotangent, ((0, 0), (0, 0), (0, extra)))
    tiles = up_cotangent.shape[2] // TILE
    chunks = kept_row.shape[0] // LANES
    row_table = jnp.asarray(interleaved_table(), jnp.bfloat16)
    lane_table = jnp.asarray(np.concatenate([hadamard(LANES)] * 2, axis=1), jnp.bfloat16)
    whole = pl.BlockSpec(memory_space=pltpu.VMEM)
    return pl.pallas_call(
        lambda *refs: sketch_kernel(row_count, column_count, tiles, *refs),
        grid=(tiles,),
        in_specs=[
            pl.BlockSpec(memory_space=pltpu.SMEM),
            whole,
            pl.BlockSpec((examples, depth, TILE), lambda j: (0, 0, j)),
            pl.BlockSpec((row_count, TILE), lambda j: (0, j)),
            whole,
            whole,
            whole,
            whole,
        ],
        out_specs=pl.BlockSpec((examples, chunks, LANES), lambda j: (0, 0, 0)),
        out_shape=jax.ShapeDtypeStruct((examples, chunks, LANES), jnp.float32),
        scratch_shapes=[
            pltpu.VMEM((examples, row_count, depth), jnp.bfloat16),
            pltpu.VMEM((row_count // LANES, 2 * LANES, TILE), jnp.float32),
            pltpu.VMEM((row_count * 2 * (column_count // LANES), LANES), jnp.float32),
            pltpu.VMEM((chunks, LANES), jnp.int32),
            pltpu.SMEM((chunks, LANES), jnp.int32),
            pltpu.VMEM((2 * LANES, LANES), jnp.float32),
            pltpu.VMEM((2 * LANES, LANES), jnp.float32),
            pltpu.SemaphoreType.DMA,
        ],
        compiler_params=pltpu.CompilerParams(vmem_limit_bytes=60 * 1024 * 1024),
    )(position, inputs, up_cotangent, signs, kept_row.reshape(chunks, LANES), kept_col.reshape(chunks, LANES),
      row_table, lane_table)


def local(inputs, up_cotangent, signs, kept_row, kept_col):
    examples = inputs.shape[0]
    position = jnp.stack([lax.axis_index("grp"), lax.axis_index("shard")]).astype(jnp.int32)
    partial = partial_features(position, inputs, up_cotangent, signs, kept_row, kept_col)
    devices = lax.axis_size("grp") * lax.axis_size("shard")
    own = kept_row.shape[0] // devices
    shares = partial.reshape(examples, devices, own).transpose(1, 0, 2)
    shares = lax.all_to_all(shares, ("grp", "shard"), 0, 0, tiled=True)
    return jnp.sum(shares, axis=0)


def solution(mesh):
    placed = (P(None, None, "grp"), P(None, None, "shard"), P("grp", "shard"), P(), P())
    return jax.shard_map(
        local, mesh=mesh, in_specs=placed, out_specs=P(None, ("grp", "shard")), check_vma=False
    )
```

time: 2600 us -> 51.3 us (0.02)
  waiting for transfers between devices: 1970 us -> 0 us
  local copies, waits for them, and re-layouts: 280 us -> 0.91 us
  matrix products: 198 us -> 0 us
  other arithmetic: 119 us -> 1.24 us
  Pallas kernels: 0 us -> 34.6 us
    ppermute x5 -> x0, waiting for transfers between devices: 1830 us -> none  [partner_2(): return lax.ppermute(block, axis, route)]
    gather x1 -> x0, local copies, waits for them, and re-layouts: 253 us -> none  [local(): jnp.take(values.reshape(examples, row_count * column_count), flat_index,...]
    dot_general x3 -> x0, matrix products: 198 us -> none  [the longest x1 115 us: local(): jnp.einsum('erc,cj->erj', values, column_table, precision=lax.Precision.H...]
    unnamed x2 -> x0, waiting for transfers between devices: 147 us -> none
    select_n x4 -> x0, other arithmetic: 67.9 us -> none  [local(): values = jnp.where(upper_half, partner - values, values + partner)]
    pallas_call x0 -> x1, Pallas kernels: none -> 34.6 us  [partial_features(): pl.pallas_call(lambda *refs: sketch_kernel(row_count, column_count, tiles...]
    dot_general x2 -> x0, other arithmetic: 34.5 us -> none  [the longest x1 23.5 us: local(): jnp.einsum('erc,cj->erj', values, column_table, precision=lax.Precision.H...]
    unnamed x13 -> x0, local copies, waits for them, and re-layouts: 27.7 us -> none
  transfers between devices with their start and end apart: 6 -> 0, of which waited for: 6 -> 0; matrix products, arithmetic and copies ran while one was open for 0% -> 0% of each run, Pallas kernels for 0% -> 0%
where the time goes in v1:
time: 51.3 us; the launch traced here: 51.1 us
  Pallas kernels  34.6 us (67%)
  blocking collectives  14.4 us (28%)
  other arithmetic  1.24 us (2%)
  local copies, waits for them, and re-layouts  0.91 us (2%)
    pallas_call x1, Pallas kernels, partial_features(): pl.pallas_call(lambda *refs: sketch_kernel(row_count, column_count, tiles...  34.6 us
    all_to_all x1, blocking collectives, local(): shares = lax.all_to_all(shares, ('grp', 'shard'), 0, 0, tiled=True)  14.4 us

profile of v1, /device:TPU:0, one launch (start us, length us, event | category | flops | bytes accessed | tf_op | source)
XLA Modules:
  0.0 51.1 jit_solution(9928514749019971140)
XLA Ops:
  0.0 0.6 %pad_add_fusion.refs_0_ = s32[2]{0:T(128)} fusion(s32[1]{0:T(128)} %bitcast.1, s32[1]{0:T(128)} %bitcast), kind=kLoop, calls=%fused_computation.1 | loop fusion | flops 2 | bytes 16 | tf_op jit(solution)/shard_map/stack | solution.py:211
  0.6 34.6 %shard_map.73 = f32[2,64,128]{2,1,0:T(8,128)} custom-call(s32[2]{0:T(128)} %pad_add_fusion.refs_0_, bf16[2,1024,1024]{2,1,0:T(8,128)(2,1)} %refs_1_.1, bf16[2,1024,1792]{2,1,0:T(8,128)(2,1)} %refs_2_.1, s32[1024,2048]{1,0:T(8,128)} %refs_3_.1, s32[64,128]{1,0:T(8,128)} %bitcast.8, s32[64,128]{1,0:T(8,128)} %bitcast.9, ...), custom_call_target="tpu_custom_call" | custom-call | tf_op jit(solution)/shard_map/pallas_call | solution.py:179
  35.2 0.9 %reshape.11 = f32[2,32,256]{2,1,0:T(8,128)S(1)} reshape(f32[2,64,128]{2,1,0:T(8,128)} %shard_map.73) | data formatting | bytes 131072 | tf_op jit(solution)/shard_map/reshape | solution.py:215
  36.1 0.1 copy.10
  36.1 14.4 %all_to_all.5 = f32[32,2,256]{2,1,0:T(2,128)S(1)} all-to-all(f32[32,2,256]{2,1,0:T(2,128)S(1)} %bitcast.7), channel_id=1, replica_groups=mesh['grp'=4,'shard'=8] {'grp','shard'}, dimensions={0} | all-to-all | bytes 131072 | tf_op jit(solution)/shard_map/all_to_all | solution.py:216
  50.5 0.6 %reduce_sum.9 = f32[2,256]{1,0:T(2,128)} reduce(f32[32,2,256]{2,1,0:T(2,128)S(1)} %all_to_all.5, f32[]{:T(128)} %constant.13.clone.1), dimensions={0}, to_apply=%region_0.0 | reduce | flops 15872 | bytes 67588 | tf_op jit(solution)/shard_map/reduce_sum | solution.py:217

commit v2 on v1

v2 whole, which is shorter than its diff:
```python
import math

import jax
import jax.numpy as jnp
import numpy as np
from jax import lax
from jax.experimental import pallas as pl
from jax.experimental.pallas import tpu as pltpu
from jax.sharding import PartitionSpec as P

D = 4096
FPAD = 16384
LANES = 128
TILE = 256
BLOCK_STRIDE = TILE + 8
X_PIECES = 2
GROUP = 4
SLOTS = 4


def hadamard(length):
    table = np.ones((1, 1), np.float32)
    while table.shape[0] < length:
        table = np.block([[table, table], [table, -table]])
    return table


def interleaved_table():
    h = hadamard(LANES)
    table = np.zeros((LANES, 2, 2, LANES), np.float32)
    table[:, 0, 0, :] = h
    table[:, 1, 1, :] = h
    return table.reshape(2 * LANES, 2 * LANES)


def butterflies(blocks):
    blocks = list(blocks)
    width = 1
    while width < len(blocks):
        for low in range(len(blocks)):
            if low & width:
                continue
            a, b = blocks[low], blocks[low | width]
            if b is None:
                blocks[low | width] = a
            else:
                blocks[low], blocks[low | width] = a + b, a - b
        width *= 2
    return blocks


def split(values):
    high = values.astype(jnp.bfloat16)
    low = (values - high.astype(jnp.float32)).astype(jnp.bfloat16)
    return high, low


def parity_sign(bits):
    for shift in (16, 8, 4, 2, 1):
        bits = jnp.bitwise_xor(bits, jnp.right_shift(bits, shift))
    return (1 - 2 * jnp.bitwise_and(bits, 1)).astype(jnp.float32)


def sketch_kernel(row_count, column_count, tiles,
                  x_ref, u_ref, signs_ref, kept_row_ref, kept_col_ref, row_table_ref, lane_table_ref,
                  out_ref,
                  x, xt, u, signs, kept_row, kept_col, row_table, lane_table,
                  product, halves, table, factor, spot_vmem, spot_smem, stages,
                  x_sem, u_sem, signs_sem, small_sem, spot_sem):
    row_blocks = row_count // LANES
    column_blocks = column_count // LANES
    pairs = column_blocks // 2
    chunks = kept_row.shape[0]
    groups = chunks // GROUP
    group_at, shard_at = lax.axis_index("grp"), lax.axis_index("shard")
    f32 = jnp.float32

    def x_copy(e, piece):
        rows = pl.ds(piece * (x.shape[1] // X_PIECES), x.shape[1] // X_PIECES)
        return pltpu.make_async_copy(x_ref.at[e, rows], x.at[e, rows], x_sem.at[e, piece])

    def columns_of(tile):
        return pl.ds(pl.multiple_of(tile * TILE, TILE), TILE)

    def u_copy(tile):
        return pltpu.make_async_copy(u_ref.at[:, :, columns_of(tile)], u.at[tile], u_sem.at[tile])

    def signs_copy(tile):
        return pltpu.make_async_copy(signs_ref.at[:, columns_of(tile)], signs.at[tile], signs_sem.at[tile])

    def spot_copy(at, slot):
        return pltpu.make_async_copy(spot_vmem.at[at], spot_smem[slot], spot_sem.at[slot])

    small = [pltpu.make_async_copy(source, target, small_sem.at[at]) for at, (source, target) in enumerate(
        [(kept_row_ref, kept_row), (kept_col_ref, kept_col), (row_table_ref, row_table), (lane_table_ref, lane_table)])]

    def ahead(tile):
        u_copy(tile).start()
        signs_copy(tile).start()

    for e in range(2):
        for piece in range(X_PIECES):
            x_copy(e, piece).start()
        if e == 0:
            ahead(0)
    for copy in small:
        copy.start()

    def place(block, column_block):
        return (block * column_blocks + column_block) * BLOCK_STRIDE

    def turn(e):
        for piece in range(X_PIECES):
            x_copy(e, piece).wait()
        for block in range(row_blocks):
            cut = slice(block * LANES, (block + 1) * LANES)
            xt[e, cut, :] = x[e, :, cut].T

    def spread(e, tile, values):
        for start in range(0, LANES, 16):
            blocks = []
            for block in range(row_blocks):
                rows = slice(block * LANES + start, block * LANES + start + 16)
                blocks.append(values[rows, :] * signs[tile, rows, :].astype(f32))
            rows = slice(e * LANES + start, e * LANES + start + 16)
            for block, mixed in enumerate(butterflies(blocks)):
                halves[block, 0, rows, :], halves[block, 1, rows, :] = split(mixed)

    def gradient(e, tile):
        return jnp.dot(xt[e], u[tile, e], preferred_element_type=f32)

    def rows_to_table(tile):
        for block in range(row_blocks):
            whole = jnp.dot(row_table[...], halves[block, 0], preferred_element_type=f32)
            whole += jnp.dot(row_table[...], halves[block, 1], preferred_element_type=f32)
            left, right = whole[:, :LANES], whole[:, LANES:]
            table[pl.ds(pl.multiple_of(place(block, 2 * tile), 8), TILE), :] = left + right
            table[pl.ds(pl.multiple_of(place(block, 2 * tile + 1), 8), TILE), :] = left - right

    turn(0)
    u_copy(0).wait()
    first = gradient(0, 0)
    signs_copy(0).wait()
    for copy in small:
        copy.wait()
    for tile in range(1, min(3, tiles)):
        ahead(tile)
    spread(0, 0, first)
    turn(1)
    product[...] = gradient(1, 0)

    row = jnp.bitwise_and(kept_row[...], row_count - 1)
    col = jnp.bitwise_and(kept_col[...], column_count - 1)
    spots = place(row // LANES, col // LANES) + jnp.bitwise_and(row, LANES - 1) * 2
    for at in range(groups):
        spot_vmem[at] = spots[at * GROUP:(at + 1) * GROUP]
    for at in range(SLOTS):
        spot_copy(at, at).start()
    factor[...] = (1.0 / math.sqrt(D * FPAD)) * parity_sign(jnp.bitwise_xor(
        jnp.bitwise_and(kept_row[...] // row_count, group_at),
        jnp.bitwise_and(kept_col[...] // column_count, shard_at)))

    def later_tile(tile, carry):
        @pl.when(tile + 2 < tiles)
        def _():
            ahead(tile + 2)

        u_copy(tile).wait()
        signs_copy(tile).wait()
        first = gradient(0, tile)
        spread(1, tile - 1, product)
        rows_to_table(tile - 1)
        second = gradient(1, tile)
        spread(0, tile, first)
        product[...] = second
        return carry

    lax.fori_loop(1, tiles, later_tile, 0)
    spread(1, tiles - 1, product)
    rows_to_table(tiles - 1)

    if pairs > 1:
        part = 32

        def columns(at, carry):
            block = at // (TILE // part)
            row = (at % (TILE // part)) * part
            base = pl.multiple_of(place(block, 0) + row, 8)
            for half in range(2):
                for extra in range(0, part, 8):
                    def rows_of(pair):
                        return pl.ds(base + (2 * pair + half) * BLOCK_STRIDE + extra, 8)

                    blocks = butterflies(
                        [table[rows_of(pair), :] if pair < tiles else None for pair in range(pairs)])
                    for pair in range(pairs):
                        table[rows_of(pair), :] = blocks[pair]
            return carry

        lax.fori_loop(0, row_blocks * (TILE // part), columns, 0)

    def gather(slot, stage):
        for part in range(GROUP):
            for u_at in range(LANES):
                at = pl.multiple_of(spot_smem[slot][part, u_at], 2)
                stage[part, 2 * u_at:2 * u_at + 2, :] = table[pl.ds(at, 2), :]

    def finish(at, stage):
        for part in range(GROUP):
            finish_chunk(at * GROUP + part, stage.at[part])

    def finish_chunk(chunk, stage):
        rows = jnp.concatenate([stage[pl.ds(0, LANES, stride=2), :], stage[pl.ds(1, LANES, stride=2), :]], axis=0)
        high, low = split(rows)
        both = jnp.concatenate([high, low], axis=1)
        whole = lax.dot_general(lane_table[...], both, (((1,), (1,)), ((), ())), preferred_element_type=f32)
        lane = jnp.bitwise_and(kept_col[pl.ds(chunk, 1), :], LANES - 1)
        sign = factor[pl.ds(chunk, 1), :]
        mask = lax.broadcasted_iota(jnp.int32, (LANES, LANES), 0) == lane
        for e in range(2):
            picked = jnp.where(mask, whole[:, e * LANES:(e + 1) * LANES], 0.0)
            out_ref[chunk, pl.ds(e, 1), :] = jnp.sum(picked, axis=0, keepdims=True) * sign

    spot_copy(0, 0).wait()
    gather(0, stages[0])
    spot_copy(min(SLOTS, groups - 1), 0).start()

    def slots_round(turn_at, carry):
        for step in range(1, SLOTS + 1):
            at = turn_at * SLOTS + step
            slot = step % SLOTS
            spot_copy(jnp.minimum(at, groups - 1), slot).wait()
            gather(slot, stages[step % 2])
            finish(at - 1, stages[(step - 1) % 2])
            spot_copy(jnp.minimum(at + SLOTS, groups - 1), slot).start()
        return carry

    lax.fori_loop(0, groups // SLOTS, slots_round, 0)
    for slot in range(SLOTS):
        spot_copy(groups - 1, slot).wait()


def partial_features(inputs, up_cotangent, signs, kept_row, kept_col):
    examples, depth, row_count = inputs.shape
    column_count = signs.shape[1]
    if up_cotangent.shape[2] % TILE:
        extra = -up_cotangent.shape[2] % TILE
        up_cotangent = jnp.pad(up_cotangent, ((0, 0), (0, 0), (0, extra)))
    tiles = up_cotangent.shape[2] // TILE
    chunks = kept_row.shape[0] // LANES
    row_table = jnp.asarray(interleaved_table(), jnp.bfloat16)
    lane_table = jnp.asarray(np.concatenate([hadamard(LANES)] * 2, axis=1), jnp.bfloat16)
    there = pl.BlockSpec(memory_space=pl.ANY)
    row_blocks = row_count // LANES
    return pl.pallas_call(
        lambda *refs: sketch_kernel(row_count, column_count, tiles, *refs),
        in_specs=[there] * 7,
        out_specs=pl.BlockSpec(memory_space=pltpu.VMEM),
        out_shape=jax.ShapeDtypeStruct((chunks, examples, LANES), jnp.float32),
        scratch_shapes=[
            pltpu.VMEM((examples, depth, row_count), jnp.bfloat16),
            pltpu.VMEM((examples, row_count, depth), jnp.bfloat16),
            pltpu.VMEM((tiles, examples, depth, TILE), jnp.bfloat16),
            pltpu.VMEM((tiles, row_count, TILE), jnp.int32),
            pltpu.VMEM((chunks, LANES), jnp.int32),
            pltpu.VMEM((chunks, LANES), jnp.int32),
            pltpu.VMEM(row_table.shape, jnp.bfloat16),
            pltpu.VMEM(lane_table.shape, jnp.bfloat16),
            pltpu.VMEM((row_count, TILE), jnp.float32),
            pltpu.VMEM((row_blocks, 2, 2 * LANES, TILE), jnp.bfloat16),
            pltpu.VMEM((row_blocks * (column_count // LANES) * BLOCK_STRIDE, LANES), jnp.float32),
            pltpu.VMEM((chunks, LANES), jnp.float32),
            pltpu.VMEM((chunks // GROUP, GROUP, LANES), jnp.int32),
            [pltpu.SMEM((GROUP, LANES), jnp.int32)] * SLOTS,
            [pltpu.VMEM((GROUP, 2 * LANES, LANES), jnp.float32)] * 2,
            pltpu.SemaphoreType.DMA((examples, X_PIECES)),
            pltpu.SemaphoreType.DMA((tiles,)),
            pltpu.SemaphoreType.DMA((tiles,)),
            pltpu.SemaphoreType.DMA((4,)),
            pltpu.SemaphoreType.DMA((SLOTS,)),
        ],
        compiler_params=pltpu.CompilerParams(vmem_limit_bytes=60 * 1024 * 1024),
    )(inputs, up_cotangent, signs, kept_row.reshape(chunks, LANES), kept_col.reshape(chunks, LANES),
      row_table, lane_table)


def local(inputs, up_cotangent, signs, kept_row, kept_col):
    examples = inputs.shape[0]
    partial = partial_features(inputs, up_cotangent, signs, kept_row, kept_col)
    devices = lax.axis_size("grp") * lax.axis_size("shard")
    own = kept_row.shape[0] // devices
    if own % LANES:
        shares = partial.transpose(1, 0, 2).reshape(examples, devices, own).transpose(1, 0, 2)
        shares = lax.all_to_all(shares, ("grp", "shard"), 0, 0, tiled=True)
        return jnp.sum(shares, axis=0)
    shares = partial.reshape(devices, own // LANES, examples, LANES)
    shares = jnp.sum(lax.all_to_all(shares, ("grp", "shard"), 0, 0, tiled=True), axis=0)
    return shares.transpose(1, 0, 2).reshape(examples, own)


def solution(mesh):
    placed = (P(None, None, "grp"), P(None, None, "shard"), P("grp", "shard"), P(), P())
    return jax.shard_map(
        local, mesh=mesh, in_specs=placed, out_specs=P(None, ("grp", "shard")), check_vma=False
    )
```

time: 51.3 us -> 47.1 us (0.918)
  Pallas kernels: 34.6 us -> 31.7 us
  local copies, waits for them, and re-layouts: 0.91 us -> 0 us
  other arithmetic: 1.24 us -> 0.62 us
    pallas_call x1, Pallas kernels: 34.6 us -> 31.7 us  [partial_features(): pl.pallas_call(lambda *refs: sketch_kernel(row_count, column_count, tiles...]
    reshape x2 -> x0, local copies, waits for them, and re-layouts: 0.91 us -> none  [local(): shares = partial.reshape(examples, devices, own).transpose(1, 0, 2)]
    another operation x1 -> x0, other arithmetic: 0.61 us -> none  [local(): jnp.stack([lax.axis_index('grp'), lax.axis_index('shard')])]
where the time goes in v2:
time: 47.1 us; the launch traced here: 46.9 us
  Pallas kernels  31.7 us (67%)
  blocking collectives  14.6 us (31%)
  other arithmetic  0.62 us (1%)
    pallas_call x1, Pallas kernels, partial_features(): pl.pallas_call(lambda *refs: sketch_kernel(row_count, column_count, tiles...  31.7 us
    all_to_all x1, blocking collectives, local(): lax.all_to_all(shares, ('grp', 'shard'), 0, 0, tiled=True)  14.6 us

profile of v2, /device:TPU:0, one launch (start us, length us, event | category | flops | bytes accessed | tf_op | source)
XLA Modules:
  0.0 46.9 jit_solution(8220530833617298065)
XLA Ops:
  0.0 31.7 %shard_map.73 = f32[64,2,128]{2,1,0:T(2,128)} custom-call(bf16[2,1024,1024]{2,1,0:T(8,128)(2,1)} %refs_0_.1, bf16[2,1024,1792]{2,1,0:T(8,128)(2,1)} %refs_1_.1, s32[1024,2048]{1,0:T(8,128)} %refs_2_.1, s32[64,128]{1,0:T(8,128)} %bitcast.7, s32[64,128]{1,0:T(8,128)} %bitcast.8, bf16[256,256]{1,0:T(8,128)(2,1)} %constant.6.clone.refs_5_, ...), custom_call_target="tpu_custom_call" | custom-call | tf_op jit(solution)/shard_map/pallas_call | solution.py:255
  31.7 14.6 %all_to_all.5 = f32[32,2,2,128]{3,2,1,0:T(2,128)S(1)} all-to-all(f32[32,2,2,128]{3,2,1,0:T(2,128)} %bitcast.6), channel_id=1, replica_groups=mesh['grp'=4,'shard'=8] {'grp','shard'}, dimensions={0} | all-to-all | bytes 131072 | tf_op jit(solution)/shard_map/all_to_all | solution.py:297
  46.3 0.6 %reduce_sum.9 = f32[2,2,128]{2,1,0:T(2,128)} reduce(f32[32,2,2,128]{3,2,1,0:T(2,128)S(1)} %all_to_all.5, f32[]{:T(128)} %constant.2.clone.1), dimensions={0}, to_apply=%region_0.0 | reduce | flops 15872 | bytes 67588 | tf_op jit(solution)/shard_map/reduce_sum | solution.py:297

commit v3 on v2

--- a/solution.py
+++ b/solution.py
@@ -12,6 +12,8 @@
 FPAD = 16384
 LANES = 128
 TILE = 256
+WIDE = 2
+SPREAD = 256
 BLOCK_STRIDE = TILE + 8
 X_PIECES = 2
 GROUP = 4
@@ -23,14 +25,6 @@
     while table.shape[0] < length:
         table = np.block([[table, table], [table, -table]])
     return table
-
-
-def interleaved_table():
-    h = hadamard(LANES)
-    table = np.zeros((LANES, 2, 2, LANES), np.float32)
-    table[:, 0, 0, :] = h
-    table[:, 1, 1, :] = h
-    return table.reshape(2 * LANES, 2 * LANES)
 
 
 def butterflies(blocks):
@@ -62,10 +56,10 @@
 
 
 def sketch_kernel(row_count, column_count, tiles,
-                  x_ref, u_ref, signs_ref, kept_row_ref, kept_col_ref, row_table_ref, lane_table_ref,
+                  x_ref, u_ref, signs_ref, kept_row_ref, kept_col_ref, twice_ref,
                   out_ref,
-                  x, xt, u, signs, kept_row, kept_col, row_table, lane_table,
-                  product, halves, table, factor, spot_vmem, spot_smem, stages,
+                  x, xt, u, signs, kept_row, kept_col, twice,
+                  halves, table, factor, spot_vmem, spot_smem, stages,
                   x_sem, u_sem, signs_sem, small_sem, spot_sem):
     row_blocks = row_count // LANES
     column_blocks = column_count // LANES
@@ -79,30 +73,38 @@
         rows = pl.ds(piece * (x.shape[1] // X_PIECES), x.shape[1] // X_PIECES)
         return pltpu.make_async_copy(x_ref.at[e, rows], x.at[e, rows], x_sem.at[e, piece])
 
-    def columns_of(tile):
-        return pl.ds(pl.multiple_of(tile * TILE, TILE), TILE)
-
-    def u_copy(tile):
-        return pltpu.make_async_copy(u_ref.at[:, :, columns_of(tile)], u.at[tile], u_sem.at[tile])
-
-    def signs_copy(tile):
-        return pltpu.make_async_copy(signs_ref.at[:, columns_of(tile)], signs.at[tile], signs_sem.at[tile])
+    first_wide = WIDE if tiles % WIDE == 0 else tiles % WIDE
+    units = u.shape[0]
+
+    def first_tile(unit):
+        return first_wide + WIDE * (unit - 1)
+
+    def u_copy(unit, tile, wide):
+        source = pl.ds(pl.multiple_of(tile * TILE, TILE), wide * TILE)
+        return pltpu.make_async_copy(
+            u_ref.at[:, :, source], u.at[unit, :, :, pl.ds(0, wide * TILE)], u_sem.at[unit])
+
+    def signs_copy(unit, tile, wide):
+        source = pl.ds(pl.multiple_of(tile * TILE, TILE), wide * TILE)
+        return pltpu.make_async_copy(
+            signs_ref.at[:, source], signs.at[unit, :, pl.ds(0, wide * TILE)], signs_sem.at[unit])
 
     def spot_copy(at, slot):
         return pltpu.make_async_copy(spot_vmem.at[at], spot_smem[slot], spot_sem.at[slot])
 
     small = [pltpu.make_async_copy(source, target, small_sem.at[at]) for at, (source, target) in enumerate(
-        [(kept_row_ref, kept_row), (kept_col_ref, kept_col), (row_table_ref, row_table), (lane_table_ref, lane_table)])]
-
-    def ahead(tile):
-        u_copy(tile).start()
-        signs_copy(tile).start()
+        [(kept_row_ref, kept_row), (kept_col_ref, kept_col), (twice_ref, twice)])]
+
+    def ahead(unit):
+        u_copy(unit, first_tile(unit), WIDE).start()
+        signs_copy(unit, first_tile(unit), WIDE).start()
 
     for e in range(2):
         for piece in range(X_PIECES):
             x_copy(e, piece).start()
         if e == 0:
-            ahead(0)
+            u_copy(0, 0, first_wide).start()
+            signs_copy(0, 0, first_wide).start()
     for copy in small:
         copy.start()
 
@@ -116,38 +118,46 @@
             cut = slice(block * LANES, (block + 1) * LANES)
             xt[e, cut, :] = x[e, :, cut].T
 
-    def spread(e, tile, values):
-        for start in range(0, LANES, 16):
-            blocks = []
-            for block in range(row_blocks):
-                rows = slice(block * LANES + start, block * LANES + start + 16)
-                blocks.append(values[rows, :] * signs[tile, rows, :].astype(f32))
-            rows = slice(e * LANES + start, e * LANES + start + 16)
-            for block, mixed in enumerate(butterflies(blocks)):
-                halves[block, 0, rows, :], halves[block, 1, rows, :] = split(mixed)
-
-    def gradient(e, tile):
-        return jnp.dot(xt[e], u[tile, e], preferred_element_type=f32)
-
-    def rows_to_table(tile):
+    def spread(e, unit, values):
+        for left in range(0, values.shape[1], SPREAD):
+            lanes = slice(left, left + SPREAD)
+            for start in range(0, LANES, 16):
+                blocks = []
+                for block in range(row_blocks):
+                    rows = slice(block * LANES + start, block * LANES + start + 16)
+                    blocks.append(values[rows, lanes] * signs[unit, rows, lanes].astype(f32))
+                for block, mixed in enumerate(butterflies(blocks)):
+                    high, low = split(mixed)
+                    halves[e][block, start:start + 16, lanes] = high
+                    halves[e][block, LANES + start:LANES + start + 16, lanes] = low
+
+    def gradient(e, unit, wide):
+        return jnp.dot(xt[e], u[unit, e, :, :wide * TILE], preferred_element_type=f32)
+
+    def rows_to_table(e, tile, wide):
         for block in range(row_blocks):
-            whole = jnp.dot(row_table[...], halves[block, 0], preferred_element_type=f32)
-            whole += jnp.dot(row_table[...], halves[block, 1], preferred_element_type=f32)
-            left, right = whole[:, :LANES], whole[:, LANES:]
-            table[pl.ds(pl.multiple_of(place(block, 2 * tile), 8), TILE), :] = left + right
-            table[pl.ds(pl.multiple_of(place(block, 2 * tile + 1), 8), TILE), :] = left - right
+            whole = jnp.dot(twice[...], halves[e][block, :, :wide * TILE], preferred_element_type=f32)
+            for at in range(wide):
+                left = whole[:, at * TILE:at * TILE + LANES]
+                right = whole[:, at * TILE + LANES:(at + 1) * TILE]
+                for half, values in enumerate((left + right, left - right)):
+                    base = pl.multiple_of(place(block, 2 * (tile + at) + half), 8)
+                    table[pl.ds(base + e, LANES, stride=2), :] = values
 
     turn(0)
-    u_copy(0).wait()
-    first = gradient(0, 0)
-    signs_copy(0).wait()
+    u_copy(0, 0, first_wide).wait()
+    first = gradient(0, 0, first_wide)
+    signs_copy(0, 0, first_wide).wait()
     for copy in small:
         copy.wait()
-    for tile in range(1, min(3, tiles)):
-        ahead(tile)
+    for unit in range(1, min(3, units)):
+        ahead(unit)
     spread(0, 0, first)
     turn(1)
-    product[...] = gradient(1, 0)
+    second = gradient(1, 0, first_wide)
+    rows_to_table(0, 0, first_wide)
+    spread(1, 0, second)
+    rows_to_table(1, 0, first_wide)
 
     row = jnp.bitwise_and(kept_row[...], row_count - 1)
     col = jnp.bitwise_and(kept_col[...], column_count - 1)
@@ -160,24 +170,23 @@
         jnp.bitwise_and(kept_row[...] // row_count, group_at),
         jnp.bitwise_and(kept_col[...] // column_count, shard_at)))
 
-    def later_tile(tile, carry):
-        @pl.when(tile + 2 < tiles)
+    def later_unit(unit, carry):
+        @pl.when(unit + 2 < units)
         def _():
-            ahead(tile + 2)
-
-        u_copy(tile).wait()
-        signs_copy(tile).wait()
-        first = gradient(0, tile)
-        spread(1, tile - 1, product)
-        rows_to_table(tile - 1)
-        second = gradient(1, tile)
-        spread(0, tile, first)
-        product[...] = second
+            ahead(unit + 2)
+
+        tile = first_tile(unit)
+        u_copy(unit, tile, WIDE).wait()
+        signs_copy(unit, tile, WIDE).wait()
+        first = gradient(0, unit, WIDE)
+        spread(0, unit, first)
+        second = gradient(1, unit, WIDE)
+        rows_to_table(0, tile, WIDE)
+        spread(1, unit, second)
+        rows_to_table(1, tile, WIDE)
         return carry
 
-    lax.fori_loop(1, tiles, later_tile, 0)
-    spread(1, tiles - 1, product)
-    rows_to_table(tiles - 1)
+    lax.fori_loop(1, units, later_unit, 0)
 
     if pairs > 1:
         part = 32
@@ -213,7 +222,7 @@
         rows = jnp.concatenate([stage[pl.ds(0, LANES, stride=2), :], stage[pl.ds(1, LANES, stride=2), :]], axis=0)
         high, low = split(rows)
         both = jnp.concatenate([high, low], axis=1)
-        whole = lax.dot_general(lane_table[...], both, (((1,), (1,)), ((), ())), preferred_element_type=f32)
+        whole = lax.dot_general(twice[...], both, (((1,), (1,)), ((), ())), preferred_element_type=f32)
         lane = jnp.bitwise_and(kept_col[pl.ds(chunk, 1), :], LANES - 1)
         sign = factor[pl.ds(chunk, 1), :]
         mask = lax.broadcasted_iota(jnp.int32, (LANES, LANES), 0) == lane
@@ -248,40 +257,38 @@
         up_cotangent = jnp.pad(up_cotangent, ((0, 0), (0, 0), (0, extra)))
     tiles = up_cotangent.shape[2] // TILE
     chunks = kept_row.shape[0] // LANES
-    row_table = jnp.asarray(interleaved_table(), jnp.bfloat16)
-    lane_table = jnp.asarray(np.concatenate([hadamard(LANES)] * 2, axis=1), jnp.bfloat16)
+    twice = jnp.asarray(np.concatenate([hadamard(LANES)] * 2, axis=1), jnp.bfloat16)
     there = pl.BlockSpec(memory_space=pl.ANY)
     row_blocks = row_count // LANES
+    units = -(-tiles // WIDE)
     return pl.pallas_call(
         lambda *refs: sketch_kernel(row_count, column_count, tiles, *refs),
-        in_specs=[there] * 7,
+        in_specs=[there] * 6,
         out_specs=pl.BlockSpec(memory_space=pltpu.VMEM),
         out_shape=jax.ShapeDtypeStruct((chunks, examples, LANES), jnp.float32),
         scratch_shapes=[
             pltpu.VMEM((examples, depth, row_count), jnp.bfloat16),
             pltpu.VMEM((examples, row_count, depth), jnp.bfloat16),
-            pltpu.VMEM((tiles, examples, depth, TILE), jnp.bfloat16),
-            pltpu.VMEM((tiles, row_count, TILE), jnp.int32),
+            pltpu.VMEM((units, examples, depth, WIDE * TILE), jnp.bfloat16),
+            pltpu.VMEM((units, row_count, WIDE * TILE), jnp.int32),
             pltpu.VMEM((chunks, LANES), jnp.int32),
             pltpu.VMEM((chunks, LANES), jnp.int32),
-            pltpu.VMEM(row_table.shape, jnp.bfloat16),
-            pltpu.VMEM(lane_table.shape, jnp.bfloat16),
-            pltpu.VMEM((row_count, TILE), jnp.float32),
-            pltpu.VMEM((row_blocks, 2, 2 * LANES, TILE), jnp.bfloat16),
+            pltpu.VMEM(twice.shape, jnp.bfloat16),
+            [pltpu.VMEM((row_blocks, 2 * LANES, WIDE * TILE), jnp.bfloat16)] * 2,
             pltpu.VMEM((row_blocks * (column_count // LANES) * BLOCK_STRIDE, LANES), jnp.float32),
             pltpu.VMEM((chunks, LANES), jnp.float32),
             pltpu.VMEM((chunks // GROUP, GROUP, LANES), jnp.int32),
             [pltpu.SMEM((GROUP, LANES), jnp.int32)] * SLOTS,
             [pltpu.VMEM((GROUP, 2 * LANES, LANES), jnp.float32)] * 2,
             pltpu.SemaphoreType.DMA((examples, X_PIECES)),
-            pltpu.SemaphoreType.DMA((tiles,)),
-            pltpu.SemaphoreType.DMA((tiles,)),
-            pltpu.SemaphoreType.DMA((4,)),
+            pltpu.SemaphoreType.DMA((units,)),
+            pltpu.SemaphoreType.DMA((units,)),
+            pltpu.SemaphoreType.DMA((3,)),
             pltpu.SemaphoreType.DMA((SLOTS,)),
         ],
         compiler_params=pltpu.CompilerParams(vmem_limit_bytes=60 * 1024 * 1024),
     )(inputs, up_cotangent, signs, kept_row.reshape(chunks, LANES), kept_col.reshape(chunks, LANES),
-      row_table, lane_table)
+      twice)
 
 
 def local(inputs, up_cotangent, signs, kept_row, kept_col):

time: 47.1 us -> 46.7 us (level)
  no operation moved by 1% of the time
where the time goes in v3:
time: 46.7 us; the launch traced here: 46.5 us
  Pallas kernels  31.3 us (67%)
  blocking collectives  14.6 us (31%)
  other arithmetic  0.62 us (1%)
    pallas_call x1, Pallas kernels, partial_features(): pl.pallas_call(lambda *refs: sketch_kernel(row_count, column_count, tiles...  31.3 us
    all_to_all x1, blocking collectives, local(): lax.all_to_all(shares, ('grp', 'shard'), 0, 0, tiled=True)  14.6 us

profile of v3, /device:TPU:0, one launch (start us, length us, event | category | flops | bytes accessed | tf_op | source)
XLA Modules:
  0.0 46.5 jit_solution(14978401703734916383)
XLA Ops:
  0.0 31.3 %shard_map.64 = f32[64,2,128]{2,1,0:T(2,128)} custom-call(bf16[2,1024,1024]{2,1,0:T(8,128)(2,1)} %refs_0_.1, bf16[2,1024,1792]{2,1,0:T(8,128)(2,1)} %refs_1_.1, s32[1024,2048]{1,0:T(8,128)} %refs_2_.1, s32[64,128]{1,0:T(8,128)} %bitcast.7, s32[64,128]{1,0:T(8,128)} %bitcast.8, bf16[128,256]{1,0:T(8,128)(2,1)} %constant.4.clone.refs_5_), custom_call_target="tpu_custom_call" | custom-call | tf_op jit(solution)/shard_map/pallas_call | solution.py:264
  31.3 14.6 %all_to_all.5 = f32[32,2,2,128]{3,2,1,0:T(2,128)S(1)} all-to-all(f32[32,2,2,128]{3,2,1,0:T(2,128)} %bitcast.6), channel_id=1, replica_groups=mesh['grp'=4,'shard'=8] {'grp','shard'}, dimensions={0} | all-to-all | bytes 131072 | tf_op jit(solution)/shard_map/all_to_all | solution.py:304
  45.9 0.6 %reduce_sum.9 = f32[2,2,128]{2,1,0:T(2,128)} reduce(f32[32,2,2,128]{3,2,1,0:T(2,128)S(1)} %all_to_all.5, f32[]{:T(128)} %constant.1.clone.1), dimensions={0}, to_apply=%region_0.0 | reduce | flops 15872 | bytes 67588 | tf_op jit(solution)/shard_map/reduce_sum | solution.py:304

commit v4 on v3

--- a/solution.py
+++ b/solution.py
@@ -16,8 +16,8 @@
 SPREAD = 256
 BLOCK_STRIDE = TILE + 8
 X_PIECES = 2
-GROUP = 4
-SLOTS = 4
+PART = 128
+STAGES = 8
 
 
 def hadamard(length):
@@ -63,9 +63,7 @@
                   x_sem, u_sem, signs_sem, small_sem, spot_sem):
     row_blocks = row_count // LANES
     column_blocks = column_count // LANES
-    pairs = column_blocks // 2
     chunks = kept_row.shape[0]
-    groups = chunks // GROUP
     group_at, shard_at = lax.axis_index("grp"), lax.axis_index("shard")
     f32 = jnp.float32
 
@@ -74,10 +72,11 @@
         return pltpu.make_async_copy(x_ref.at[e, rows], x.at[e, rows], x_sem.at[e, piece])
 
     first_wide = WIDE if tiles % WIDE == 0 else tiles % WIDE
+    last = tiles - first_wide
     units = u.shape[0]
 
     def first_tile(unit):
-        return first_wide + WIDE * (unit - 1)
+        return WIDE * (unit - 1)
 
     def u_copy(unit, tile, wide):
         source = pl.ds(pl.multiple_of(tile * TILE, TILE), wide * TILE)
@@ -89,8 +88,7 @@
         return pltpu.make_async_copy(
             signs_ref.at[:, source], signs.at[unit, :, pl.ds(0, wide * TILE)], signs_sem.at[unit])
 
-    def spot_copy(at, slot):
-        return pltpu.make_async_copy(spot_vmem.at[at], spot_smem[slot], spot_sem.at[slot])
+    spot_copy = pltpu.make_async_copy(spot_vmem, spot_smem, spot_sem)
 
     small = [pltpu.make_async_copy(source, target, small_sem.at[at]) for at, (source, target) in enumerate(
         [(kept_row_ref, kept_row), (kept_col_ref, kept_col), (twice_ref, twice)])]
@@ -103,8 +101,8 @@
         for piece in range(X_PIECES):
             x_copy(e, piece).start()
         if e == 0:
-            u_copy(0, 0, first_wide).start()
-            signs_copy(0, 0, first_wide).start()
+            u_copy(0, last, first_wide).start()
+            signs_copy(0, last, first_wide).start()
     for copy in small:
         copy.start()
 
@@ -137,17 +135,15 @@
     def rows_to_table(e, tile, wide):
         for block in range(row_blocks):
             whole = jnp.dot(twice[...], halves[e][block, :, :wide * TILE], preferred_element_type=f32)
-            for at in range(wide):
-                left = whole[:, at * TILE:at * TILE + LANES]
-                right = whole[:, at * TILE + LANES:(at + 1) * TILE]
-                for half, values in enumerate((left + right, left - right)):
-                    base = pl.multiple_of(place(block, 2 * (tile + at) + half), 8)
-                    table[pl.ds(base + e, LANES, stride=2), :] = values
+            parts = butterflies([whole[:, at:at + LANES] for at in range(0, wide * TILE, LANES)])
+            for at, values in enumerate(parts):
+                base = pl.multiple_of(place(block, 2 * tile + at), 8)
+                table[pl.ds(base + e, LANES, stride=2), :] = values
 
     turn(0)
-    u_copy(0, 0, first_wide).wait()
+    u_copy(0, last, first_wide).wait()
     first = gradient(0, 0, first_wide)
-    signs_copy(0, 0, first_wide).wait()
+    signs_copy(0, last, first_wide).wait()
     for copy in small:
         copy.wait()
     for unit in range(1, min(3, units)):
@@ -155,17 +151,14 @@
     spread(0, 0, first)
     turn(1)
     second = gradient(1, 0, first_wide)
-    rows_to_table(0, 0, first_wide)
+    rows_to_table(0, last, first_wide)
     spread(1, 0, second)
-    rows_to_table(1, 0, first_wide)
+    rows_to_table(1, last, first_wide)
 
     row = jnp.bitwise_and(kept_row[...], row_count - 1)
     col = jnp.bitwise_and(kept_col[...], column_count - 1)
-    spots = place(row // LANES, col // LANES) + jnp.bitwise_and(row, LANES - 1) * 2
-    for at in range(groups):
-        spot_vmem[at] = spots[at * GROUP:(at + 1) * GROUP]
-    for at in range(SLOTS):
-        spot_copy(at, at).start()
+    spot_vmem[...] = place(row // LANES, col // LANES) + jnp.bitwise_and(row, LANES - 1) * 2
+    spot_copy.start()
     factor[...] = (1.0 / math.sqrt(D * FPAD)) * parity_sign(jnp.bitwise_xor(
         jnp.bitwise_and(kept_row[...] // row_count, group_at),
         jnp.bitwise_and(kept_col[...] // column_count, shard_at)))
@@ -188,65 +181,55 @@
 
     lax.fori_loop(1, units, later_unit, 0)
 
-    if pairs > 1:
-        part = 32
-
+    quads = column_blocks // (2 * WIDE)
+    if quads > 1:
         def columns(at, carry):
-            block = at // (TILE // part)
-            row = (at % (TILE // part)) * part
+            block = at // (TILE // PART)
+            row = (at % (TILE // PART)) * PART
             base = pl.multiple_of(place(block, 0) + row, 8)
-            for half in range(2):
-                for extra in range(0, part, 8):
-                    def rows_of(pair):
-                        return pl.ds(base + (2 * pair + half) * BLOCK_STRIDE + extra, 8)
-
-                    blocks = butterflies(
-                        [table[rows_of(pair), :] if pair < tiles else None for pair in range(pairs)])
-                    for pair in range(pairs):
-                        table[rows_of(pair), :] = blocks[pair]
+            for extra in range(0, PART, 8):
+                def rows_of(quad, inner):
+                    return pl.ds(base + (2 * WIDE * quad + inner) * BLOCK_STRIDE + extra, 8)
+
+                loaded = {}
+                for inner in range(2 * WIDE):
+                    blocks = []
+                    for quad in range(quads):
+                        present = min(max(tiles - WIDE * quad, 0), WIDE) * 2
+                        if present:
+                            key = quad, inner % present
+                            if key not in loaded:
+                                loaded[key] = table[rows_of(*key), :]
+                        blocks.append(loaded[key] if present else None)
+                    blocks = butterflies(blocks)
+                    for quad in range(quads):
+                        table[rows_of(quad, inner), :] = blocks[quad]
             return carry
 
-        lax.fori_loop(0, row_blocks * (TILE // part), columns, 0)
-
-    def gather(slot, stage):
-        for part in range(GROUP):
-            for u_at in range(LANES):
-                at = pl.multiple_of(spot_smem[slot][part, u_at], 2)
-                stage[part, 2 * u_at:2 * u_at + 2, :] = table[pl.ds(at, 2), :]
-
-    def finish(at, stage):
-        for part in range(GROUP):
-            finish_chunk(at * GROUP + part, stage.at[part])
+        lax.fori_loop(0, row_blocks * (TILE // PART), columns, 0)
+
+    def gather(chunk, stage):
+        for u_at in range(LANES):
+            at = pl.multiple_of(spot_smem[chunk, u_at], 2)
+            stage[2 * u_at:2 * u_at + 2, :] = table[pl.ds(at, 2), :]
 
     def finish_chunk(chunk, stage):
-        rows = jnp.concatenate([stage[pl.ds(0, LANES, stride=2), :], stage[pl.ds(1, LANES, stride=2), :]], axis=0)
-        high, low = split(rows)
-        both = jnp.concatenate([high, low], axis=1)
-        whole = lax.dot_general(twice[...], both, (((1,), (1,)), ((), ())), preferred_element_type=f32)
-        lane = jnp.bitwise_and(kept_col[pl.ds(chunk, 1), :], LANES - 1)
-        sign = factor[pl.ds(chunk, 1), :]
-        mask = lax.broadcasted_iota(jnp.int32, (LANES, LANES), 0) == lane
+        col = jnp.broadcast_to(kept_col[pl.ds(chunk, 1), :], (8, LANES))
+        flips = [(1 - 2 * jnp.bitwise_and(jnp.right_shift(col, bit), 1)).astype(f32) for bit in range(3, 7)]
+        bits = jnp.bitwise_and(col, lax.broadcasted_iota(jnp.int32, (8, LANES), 0))
+        bits = jnp.bitwise_xor(bits, jnp.bitwise_xor(jnp.right_shift(bits, 1), jnp.right_shift(bits, 2)))
+        weights = (1 - 2 * jnp.bitwise_and(bits, 1)).astype(f32) * factor[pl.ds(chunk, 1), :]
         for e in range(2):
-            picked = jnp.where(mask, whole[:, e * LANES:(e + 1) * LANES], 0.0)
-            out_ref[chunk, pl.ds(e, 1), :] = jnp.sum(picked, axis=0, keepdims=True) * sign
-
-    spot_copy(0, 0).wait()
-    gather(0, stages[0])
-    spot_copy(min(SLOTS, groups - 1), 0).start()
-
-    def slots_round(turn_at, carry):
-        for step in range(1, SLOTS + 1):
-            at = turn_at * SLOTS + step
-            slot = step % SLOTS
-            spot_copy(jnp.minimum(at, groups - 1), slot).wait()
-            gather(slot, stages[step % 2])
-            finish(at - 1, stages[(step - 1) % 2])
-            spot_copy(jnp.minimum(at + SLOTS, groups - 1), slot).start()
-        return carry
-
-    lax.fori_loop(0, groups // SLOTS, slots_round, 0)
-    for slot in range(SLOTS):
-        spot_copy(groups - 1, slot).wait()
+            turned = stage[pl.ds(e, LANES, stride=2), :].T
+            parts = [turned[start:start + 8] for start in range(0, LANES, 8)]
+            for flip in flips:
+                parts = [low + high * flip for low, high in zip(parts[0::2], parts[1::2])]
+            out_ref[chunk, pl.ds(e, 1), :] = jnp.sum(parts[0] * weights, axis=0, keepdims=True)
+
+    spot_copy.wait()
+    for chunk in range(chunks):
+        gather(chunk, stages[chunk % len(stages)])
+        finish_chunk(chunk, stages[chunk % len(stages)])
 
 
 def partial_features(inputs, up_cotangent, signs, kept_row, kept_col):
@@ -277,14 +260,14 @@
             [pltpu.VMEM((row_blocks, 2 * LANES, WIDE * TILE), jnp.bfloat16)] * 2,
             pltpu.VMEM((row_blocks * (column_count // LANES) * BLOCK_STRIDE, LANES), jnp.float32),
             pltpu.VMEM((chunks, LANES), jnp.float32),
-            pltpu.VMEM((chunks // GROUP, GROUP, LANES), jnp.int32),
-            [pltpu.SMEM((GROUP, LANES), jnp.int32)] * SLOTS,
-            [pltpu.VMEM((GROUP, 2 * LANES, LANES), jnp.float32)] * 2,
+            pltpu.VMEM((chunks, LANES), jnp.int32),
+            pltpu.SMEM((chunks, LANES), jnp.int32),
+            [pltpu.VMEM((2 * LANES, LANES), jnp.float32)] * STAGES,
             pltpu.SemaphoreType.DMA((examples, X_PIECES)),
             pltpu.SemaphoreType.DMA((units,)),
             pltpu.SemaphoreType.DMA((units,)),
             pltpu.SemaphoreType.DMA((3,)),
-            pltpu.SemaphoreType.DMA((SLOTS,)),
+            pltpu.SemaphoreType.DMA,
         ],
         compiler_params=pltpu.CompilerParams(vmem_limit_bytes=60 * 1024 * 1024),
     )(inputs, up_cotangent, signs, kept_row.reshape(chunks, LANES), kept_col.reshape(chunks, LANES),

time: 46.7 us -> 42.8 us (0.916)
  Pallas kernels: 31.3 us -> 27.4 us
    pallas_call x1, Pallas kernels: 31.3 us -> 27.4 us  [partial_features(): pl.pallas_call(lambda *refs: sketch_kernel(row_count, column_count, tiles...]
where the time goes in v4:
time: 42.8 us; the launch traced here: 42.7 us
  Pallas kernels  27.4 us (64%)
  blocking collectives  14.6 us (34%)
  other arithmetic  0.62 us (1%)
    pallas_call x1, Pallas kernels, partial_features(): pl.pallas_call(lambda *refs: sketch_kernel(row_count, column_count, tiles...  27.4 us
    all_to_all x1, blocking collectives, local(): lax.all_to_all(shares, ('grp', 'shard'), 0, 0, tiled=True)  14.6 us

profile of v4, /device:TPU:0, one launch (start us, length us, event | category | flops | bytes accessed | tf_op | source)
XLA Modules:
  0.0 42.7 jit_solution(13775069881134293790)
XLA Ops:
  0.0 27.4 %shard_map.64 = f32[64,2,128]{2,1,0:T(2,128)} custom-call(bf16[2,1024,1024]{2,1,0:T(8,128)(2,1)} %refs_0_.1, bf16[2,1024,1792]{2,1,0:T(8,128)(2,1)} %refs_1_.1, s32[1024,2048]{1,0:T(8,128)} %refs_2_.1, s32[64,128]{1,0:T(8,128)} %bitcast.7, s32[64,128]{1,0:T(8,128)} %bitcast.8, bf16[128,256]{1,0:T(8,128)(2,1)} %constant.4.clone.refs_5_), custom_call_target="tpu_custom_call" | custom-call | tf_op jit(solution)/shard_map/pallas_call | solution.py:247
  27.5 14.6 %all_to_all.5 = f32[32,2,2,128]{3,2,1,0:T(2,128)S(1)} all-to-all(f32[32,2,2,128]{3,2,1,0:T(2,128)} %bitcast.6), channel_id=1, replica_groups=mesh['grp'=4,'shard'=8] {'grp','shard'}, dimensions={0} | all-to-all | bytes 131072 | tf_op jit(solution)/shard_map/all_to_all | solution.py:287
  42.0 0.6 %reduce_sum.9 = f32[2,2,128]{2,1,0:T(2,128)} reduce(f32[32,2,2,128]{3,2,1,0:T(2,128)S(1)} %all_to_all.5, f32[]{:T(128)} %constant.1.clone.1), dimensions={0}, to_apply=%region_0.0 | reduce | flops 15872 | bytes 67588 | tf_op jit(solution)/shard_map/reduce_sum | solution.py:287

commit v5 on v4

--- a/solution.py
+++ b/solution.py
@@ -15,7 +15,7 @@
 WIDE = 2
 SPREAD = 256
 BLOCK_STRIDE = TILE + 8
-X_PIECES = 2
+X_PIECES = 4
 PART = 128
 STAGES = 8
 
@@ -110,24 +110,22 @@
         return (block * column_blocks + column_block) * BLOCK_STRIDE
 
     def turn(e):
-        for piece in range(X_PIECES):
-            x_copy(e, piece).wait()
         for block in range(row_blocks):
             cut = slice(block * LANES, (block + 1) * LANES)
             xt[e, cut, :] = x[e, :, cut].T
 
-    def spread(e, unit, values):
-        for left in range(0, values.shape[1], SPREAD):
+    def spread(unit, both):
+        for left in range(0, both[0].shape[1], SPREAD):
             lanes = slice(left, left + SPREAD)
             for start in range(0, LANES, 16):
-                blocks = []
-                for block in range(row_blocks):
-                    rows = slice(block * LANES + start, block * LANES + start + 16)
-                    blocks.append(values[rows, lanes] * signs[unit, rows, lanes].astype(f32))
-                for block, mixed in enumerate(butterflies(blocks)):
-                    high, low = split(mixed)
-                    halves[e][block, start:start + 16, lanes] = high
-                    halves[e][block, LANES + start:LANES + start + 16, lanes] = low
+                places = [slice(block * LANES + start, block * LANES + start + 16) for block in range(row_blocks)]
+                coins = [signs[unit, rows, lanes].astype(f32) for rows in places]
+                for e in range(2):
+                    blocks = butterflies([both[e][rows, lanes] * coin for rows, coin in zip(places, coins)])
+                    for block, mixed in enumerate(blocks):
+                        high, low = split(mixed)
+                        halves[e][block, start:start + 16, lanes] = high
+                        halves[e][block, LANES + start:LANES + start + 16, lanes] = low
 
     def gradient(e, unit, wide):
         return jnp.dot(xt[e], u[unit, e, :, :wide * TILE], preferred_element_type=f32)
@@ -140,20 +138,22 @@
                 base = pl.multiple_of(place(block, 2 * tile + at), 8)
                 table[pl.ds(base + e, LANES, stride=2), :] = values
 
-    turn(0)
+    for e in range(2):
+        for piece in range(X_PIECES):
+            x_copy(e, piece).wait()
     u_copy(0, last, first_wide).wait()
-    first = gradient(0, 0, first_wide)
-    signs_copy(0, last, first_wide).wait()
     for copy in small:
         copy.wait()
+    signs_copy(0, last, first_wide).wait()
     for unit in range(1, min(3, units)):
         ahead(unit)
-    spread(0, 0, first)
+    turn(0)
+    first = gradient(0, 0, first_wide)
     turn(1)
     second = gradient(1, 0, first_wide)
-    rows_to_table(0, last, first_wide)
-    spread(1, 0, second)
-    rows_to_table(1, last, first_wide)
+    spread(0, (first, second))
+    for e in range(2):
+        rows_to_table(e, last, first_wide)
 
     row = jnp.bitwise_and(kept_row[...], row_count - 1)
     col = jnp.bitwise_and(kept_col[...], column_count - 1)
@@ -172,11 +172,10 @@
         u_copy(unit, tile, WIDE).wait()
         signs_copy(unit, tile, WIDE).wait()
         first = gradient(0, unit, WIDE)
-        spread(0, unit, first)
         second = gradient(1, unit, WIDE)
-        rows_to_table(0, tile, WIDE)
-        spread(1, unit, second)
-        rows_to_table(1, tile, WIDE)
+        spread(unit, (first, second))
+        for e in range(2):
+            rows_to_table(e, tile, WIDE)
         return carry
 
     lax.fori_loop(1, units, later_unit, 0)

time: 42.8 us -> 42.1 us (0.984)
  Pallas kernels: 27.4 us -> 26.8 us
    pallas_call x1, Pallas kernels: 27.4 us -> 26.8 us  [partial_features(): pl.pallas_call(lambda *refs: sketch_kernel(row_count, column_count, tiles...]
where the time goes in v5:
time: 42.1 us; the launch traced here: 42 us
  Pallas kernels  26.8 us (64%)
  blocking collectives  14.6 us (35%)
  other arithmetic  0.62 us (1%)
    pallas_call x1, Pallas kernels, partial_features(): pl.pallas_call(lambda *refs: sketch_kernel(row_count, column_count, tiles...  26.8 us
    all_to_all x1, blocking collectives, local(): lax.all_to_all(shares, ('grp', 'shard'), 0, 0, tiled=True)  14.6 us

profile of v5, /device:TPU:0, one launch (start us, length us, event | category | flops | bytes accessed | tf_op | source)
XLA Modules:
  0.0 42.0 jit_solution(14652335269232819253)
XLA Ops:
  0.0 26.8 %shard_map.64 = f32[64,2,128]{2,1,0:T(2,128)} custom-call(bf16[2,1024,1024]{2,1,0:T(8,128)(2,1)} %refs_0_.1, bf16[2,1024,1792]{2,1,0:T(8,128)(2,1)} %refs_1_.1, s32[1024,2048]{1,0:T(8,128)} %refs_2_.1, s32[64,128]{1,0:T(8,128)} %bitcast.7, s32[64,128]{1,0:T(8,128)} %bitcast.8, bf16[128,256]{1,0:T(8,128)(2,1)} %constant.4.clone.refs_5_), custom_call_target="tpu_custom_call" | custom-call | tf_op jit(solution)/shard_map/pallas_call | solution.py:246
  26.8 14.6 %all_to_all.5 = f32[32,2,2,128]{3,2,1,0:T(2,128)S(1)} all-to-all(f32[32,2,2,128]{3,2,1,0:T(2,128)} %bitcast.6), channel_id=1, replica_groups=mesh['grp'=4,'shard'=8] {'grp','shard'}, dimensions={0} | all-to-all | bytes 131072 | tf_op jit(solution)/shard_map/all_to_all | solution.py:286
  41.3 0.6 %reduce_sum.9 = f32[2,2,128]{2,1,0:T(2,128)} reduce(f32[32,2,2,128]{3,2,1,0:T(2,128)S(1)} %all_to_all.5, f32[]{:T(128)} %constant.1.clone.1), dimensions={0}, to_apply=%region_0.0 | reduce | flops 15872 | bytes 67588 | tf_op jit(solution)/shard_map/reduce_sum | solution.py:286
